TPU v7x, 256 devices: a whole 4x4x8 slice. The times are simulated.
256 devices in a mesh: ctx: 32 (over y, x, core), head: 8 (over z).
Axes of the slice: x: 4, y: 4, z: 8, core: 2. Of those that a mesh axis runs over, the one named last changes fastest.
Arguments:
- queries: bfloat16 [4096, 128, 576], P('ctx', 'head'), may hold values from -6 to 6
- out_grads: bfloat16 [4096, 128, 512], P('ctx', 'head'), may hold values from -6 to 6
- latent: bfloat16 [16384, 576], P('ctx'), may hold values from -6 to 6
- block_lists: int32 [64, 16], P('ctx'), may hold values from 0 to 255, as said below
- block_home: int32 [256], replicated, may hold values from 0 to 255, as said below
Outputs:
- query_grads: bfloat16 [4096, 128, 576], P('ctx', 'head')
- latent_grads: float32 [16384, 576], P('ctx')
Inputs may be any that keep to these rules, and one draw needn't show every extreme that they name: Block b is stored at rows block_home[b]*64 to block_home[b]*64 + 63 of latent; block_home is a permutation. `block_lists`: each row names distinct blocks. Among the 32 entries of the rows of one index of ctx, at most 2 name blocks whose block_home lies in one range o*8 to o*8 + 7, and some range is named exactly 2 times.
All inputs are finite; a program needn't handle non-finite values.
Results may differ from a plain program's by a relative error of at most 0.0058.
Values may be sent and summed in bfloat16 or wider, within the bound.
No kernel may reach another device: no remote copies, remote signals or barrier semaphores. Data moves between devices by JAX's collectives and lax.ppermute only.
A program may use at most 128 MiB of HBM per device.

v0:
```python
import functools

import jax
import jax.numpy as jnp
from jax import lax
from jax.experimental import pallas as pl
from jax.experimental.pallas import tpu as pltpu
from jax.sharding import PartitionSpec as P

BLK = 64
CAPACITY = 2
LOG2E = 1.4426950408889634
softmax_scale = 192.0 ** (-0.5)
LARGE_LIMIT = 56 * 1024 * 1024
SMALL_LIMIT = 16 * 1024 * 1024
ROWS_BY_ROWS = (((1,), (1,)), ((), ()))
COLS_BY_COLS = (((0,), (0,)), ((), ()))
OFFSETS = (0, 1, -1, 2, -2, 3, -3, 4)


def smem():
    return pl.BlockSpec(memory_space=pltpu.SMEM)


def vmem():
    return pl.BlockSpec(memory_space=pltpu.VMEM)


def one_hot(hit):
    return jnp.where(hit, 1.0, 0.0).astype(jnp.bfloat16)


def plan_kernel(stored_blocks, lists_ref, home_ref, entry_ref, count):
    groups, chosen = lists_ref.shape
    for owner in range(count.shape[0]):
        count[owner] = 0
    for slot in range(entry_ref.shape[0]):
        entry_ref[slot] = 0
    for group in range(groups):
        for at in range(chosen):
            owner = home_ref[lists_ref[group, at]] // stored_blocks
            earlier = count[owner]
            entry_ref[owner * CAPACITY + earlier] = group * chosen + at
            count[owner] = earlier + 1


def plan(block_lists, block_home, ctx_count, stored_blocks):
    return pl.pallas_call(
        functools.partial(plan_kernel, stored_blocks),
        out_shape=jax.ShapeDtypeStruct((ctx_count * CAPACITY,), jnp.int32),
        in_specs=[smem(), smem()],
        out_specs=smem(),
        scratch_shapes=[pltpu.SMEM((ctx_count,), jnp.int32)],
        name="plan",
    )(block_lists, block_home)


def spread_kernel(pair, lists_ref, home_ref, latent_ref, out_ref):
    width, tokens = latent_ref.shape
    stored = tokens // BLK
    span = stored * pair
    row = lax.broadcasted_iota(jnp.int32, (tokens, tokens), 0)
    col = lax.broadcasted_iota(jnp.int32, (tokens, tokens), 1)
    source = (row % span) // pair * BLK + row // span * pair + row % pair
    moved = lax.dot_general(
        one_hot(col == source),
        latent_ref[...],
        ROWS_BY_ROWS,
        preferred_element_type=jnp.float32,
    )
    out_ref[:, :width] = moved.astype(out_ref.dtype)
    free = out_ref.shape[1] - width
    entry = lax.broadcasted_iota(jnp.int32, (span, free), 0) // pair
    entry = entry + stored * lax.broadcasted_iota(jnp.int32, (span, free), 1)
    groups, chosen = lists_ref.shape
    value = jnp.zeros((span, free), jnp.float32)
    for group in range(groups):
        for at in range(chosen):
            position = home_ref[lists_ref[group, at]].astype(jnp.float32)
            value = jnp.where(entry == group * chosen + at, position, value)
    value = value.astype(out_ref.dtype)
    for start in range(0, tokens, span):
        out_ref[start : start + span, width:] = value


def spread(block_lists, block_home, latent_cols, pair):
    width, tokens = latent_cols.shape
    return pl.pallas_call(
        functools.partial(spread_kernel, pair),
        out_shape=jax.ShapeDtypeStruct((tokens, 640), latent_cols.dtype),
        in_specs=[smem(), smem(), vmem()],
        out_specs=vmem(),
        compiler_params=pltpu.CompilerParams(vmem_limit_bytes=LARGE_LIMIT),
        name="spread",
    )(block_lists, block_home, latent_cols)


def choose_kernel(pair, held_ref, *out_refs):
    targets, _, width = out_refs[0].shape
    count = held_ref.shape[0]
    span = count // targets
    steps = out_refs[0].shape[1] // span
    rows = held_ref[:, :width]
    lists = held_ref[:, width:].astype(jnp.float32)
    parity = lax.broadcasted_iota(jnp.int32, (count, 1), 0) % pair
    col = lax.broadcasted_iota(jnp.int32, (count, count), 1).astype(jnp.float32)
    for group, out_ref in enumerate(out_refs):
        for step in range(steps):
            at = group * steps + step
            source = lists[:, at : at + 1] * pair + parity.astype(jnp.float32)
            chosen = jnp.dot(one_hot(col == source), rows, preferred_element_type=jnp.float32)
            chosen = chosen.astype(out_ref.dtype).reshape(targets, span, width)
            out_ref[:, step * span : (step + 1) * span] = chosen


def choose(held, width, targets, groups, chosen, pair):
    one = jax.ShapeDtypeStruct((targets, chosen * pair, width), held.dtype)
    return pl.pallas_call(
        functools.partial(choose_kernel, pair),
        out_shape=[one] * groups,
        in_specs=[vmem()],
        out_specs=[vmem()] * groups,
        compiler_params=pltpu.CompilerParams(vmem_limit_bytes=SMALL_LIMIT),
        name="choose",
    )(held)


def place_kernel(pair, index_ref, *refs):
    term_refs, out_ref, total, picks = refs[:-3], refs[-3], refs[-2], refs[-1]
    half = len(term_refs) // 2
    rows = term_refs[0].shape[0]
    share = out_ref.shape[1]
    spread_over = rows * pair // share
    for group in range(2):
        terms = term_refs[group * half : (group + 1) * half]
        value = terms[0][...].astype(jnp.float32)
        for term in terms[1:]:
            value = value + term[...].astype(jnp.float32)
        total[group * rows : (group + 1) * rows, :] = value.astype(total.dtype)
    row = lax.broadcasted_iota(jnp.int32, (share, 2 * rows), 0)
    col = lax.broadcasted_iota(jnp.int32, (share, 2 * rows), 1)
    lead = col - (row // pair * spread_over + row % pair)
    chosen = spread_over // pair

    def one_slot(slot, carry):
        entry = index_ref[slot]
        start = entry // chosen * rows + entry % chosen * pair
        at = pl.multiple_of(slot * share, share)
        picks[pl.ds(at, share), :] = jnp.where(lead == start, 1.0, 0.0)
        return carry

    lax.fori_loop(0, out_ref.shape[0], one_slot, 0, unroll=4)
    placed = jnp.dot(
        picks[...].astype(jnp.bfloat16), total[...], preferred_element_type=jnp.float32
    )
    out_ref[...] = placed.astype(out_ref.dtype).reshape(out_ref.shape)


def place(index, by_group, share, pair):
    terms = [term for group in by_group for term in group]
    rows, width = terms[0].shape
    slots = index.shape[0]
    return pl.pallas_call(
        functools.partial(place_kernel, pair),
        out_shape=jax.ShapeDtypeStruct((slots, share, width), jnp.bfloat16),
        in_specs=[smem()] + [vmem()] * len(terms),
        out_specs=vmem(),
        scratch_shapes=[
            pltpu.VMEM((2 * rows, width), jnp.bfloat16),
            pltpu.VMEM((slots * share, 2 * rows), jnp.float32),
        ],
        compiler_params=pltpu.CompilerParams(vmem_limit_bytes=SMALL_LIMIT),
        name="place",
    )(index, *terms)


def gather_sum_kernel(index_ref, rows_ref, out_ref, total):
    total[...] = jnp.zeros_like(total)
    stored = out_ref.shape[0]

    def one_slot(at, carry):
        index = index_ref[at]
        index = jnp.where(index < 0, stored, index)
        total[index] += rows_ref[at].astype(jnp.float32)
        return carry

    lax.fori_loop(0, rows_ref.shape[0], one_slot, 0, unroll=4)
    out_ref[...] = total[:stored].astype(out_ref.dtype)


def gather_sum(index, rows, stored):
    return pl.pallas_call(
        gather_sum_kernel,
        out_shape=jax.ShapeDtypeStruct((stored,) + rows.shape[1:], jnp.bfloat16),
        in_specs=[smem(), vmem()],
        out_specs=vmem(),
        scratch_shapes=[pltpu.VMEM((stored + 1,) + rows.shape[1:], jnp.float32)],
        compiler_params=pltpu.CompilerParams(vmem_limit_bytes=SMALL_LIMIT),
        name="gather_sum",
    )(index, rows)


def each(count, total, do):
    if count == 1:
        do(slice(None))
        return
    size = total // count

    def one(at, carry):
        do(pl.ds(pl.multiple_of(at * size, size), size))
        return carry

    lax.fori_loop(0, count, one, 0)


def group_kernel(pieces, me_ref, key_ref, query_ref, grad_ref, query_out, *refs):
    part_refs, (sums, halves, score_halves) = refs[:-3], refs[-3:]
    rows, width = query_ref.shape
    value_width = grad_ref.shape[1]
    keys = key_ref[...].reshape(sums.shape)

    def weigh(cols):
        scores = lax.dot_general(
            keys, query_ref[cols, :], ROWS_BY_ROWS, preferred_element_type=jnp.float32
        )
        factor = softmax_scale * LOG2E
        top = jnp.max(scores, axis=0, keepdims=True) * factor
        raised = jnp.exp2(scores * factor - top)
        weights = raised * (1.0 / jnp.sum(raised, axis=0, keepdims=True))
        half = weights.astype(jnp.bfloat16)
        weight_grad = lax.dot_general(
            keys[:, :value_width],
            grad_ref[cols, :],
            ROWS_BY_ROWS,
            preferred_element_type=jnp.float32,
        )
        delta = jnp.sum(half.astype(jnp.float32) * weight_grad, axis=0, keepdims=True)
        halves[:, cols] = half
        score_halves[:, cols] = (weights * (weight_grad - delta)).astype(jnp.bfloat16)

    def key_sums(at):
        from_scores = (
            jnp.dot(score_halves[at, :], query_ref[...], preferred_element_type=jnp.float32)
            * softmax_scale
        )
        from_values = jnp.dot(halves[at, :], grad_ref[...], preferred_element_type=jnp.float32)
        sums[at, :value_width] = from_scores[:, :value_width] + from_values
        sums[at, value_width:] = from_scores[:, value_width:]

    def query_sums(cols):
        query_out[:, cols] = (
            lax.dot_general(
                keys, score_halves[:, cols], COLS_BY_COLS, preferred_element_type=jnp.float32
            )
            * softmax_scale
        ).astype(jnp.bfloat16)

    each(pieces, rows, weigh)
    each(pieces, sums.shape[0], key_sums)
    each(pieces, rows, query_sums)

    me = me_ref[0]
    count = len(OFFSETS)
    part = sums.shape[0] // count
    for out, offset in zip(part_refs, OFFSETS):
        start = pl.multiple_of((me + offset + count) % count * part, part)
        out[...] = sums[pl.ds(start, part), :].astype(out.dtype)


def group_grads(group, pieces, me, keys, query_rows, grad_rows):
    key_count = keys.shape[0] * keys.shape[1]
    width = keys.shape[2]
    rows, value_width = grad_rows.shape[1:]
    part = key_count // len(OFFSETS)
    by_group = lambda *shape: pl.BlockSpec((None,) + shape, lambda i: (group, 0, 0))
    whole = lambda *shape: pl.BlockSpec(shape, lambda i: (0,) * len(shape))
    out_shape = [jax.ShapeDtypeStruct((width, rows), jnp.bfloat16)]
    for offset in OFFSETS:
        kind = jnp.float32 if offset == 0 else jnp.bfloat16
        out_shape.append(jax.ShapeDtypeStruct((part, width), kind))
    flops = 2 * rows * key_count * (3 * width + 2 * value_width)
    return pl.pallas_call(
        functools.partial(group_kernel, pieces),
        grid=(1,),
        in_specs=[
            smem(),
            whole(*keys.shape),
            by_group(rows, width),
            by_group(rows, value_width),
        ],
        out_specs=[whole(*shape.shape) for shape in out_shape],
        out_shape=out_shape,
        scratch_shapes=[
            pltpu.VMEM((key_count, width), jnp.float32),
            pltpu.VMEM((key_count, rows), jnp.bfloat16),
            pltpu.VMEM((key_count, rows), jnp.bfloat16),
        ],
        compiler_params=pltpu.CompilerParams(vmem_limit_bytes=LARGE_LIMIT),
        cost_estimate=pl.CostEstimate(
            flops=flops, bytes_accessed=8_000_000, transcendentals=rows * key_count
        ),
        name="group_grads",
    )(me, keys, query_rows, grad_rows)


def shift(x, by):
    count = lax.axis_size("head")
    return lax.ppermute(x, "head", [(i, (i + by) % count) for i in range(count)])


def add(a, b):
    return (a.astype(jnp.float32) + b.astype(jnp.float32)).astype(jnp.bfloat16)


def ring_start(parts):
    return shift(parts[4], 1), shift(parts[-3], -1)


def ring_end(parts, right, left):
    right, left = shift(add(parts[3], right), 1), shift(add(parts[-2], left), -1)
    right, left = shift(add(parts[2], right), 1), shift(add(parts[-1], left), -1)
    return parts[0], shift(add(parts[1], right), 1), left


def ring_whole(parts):
    right, left = shift(parts[3], 1), shift(parts[4], -1)
    right, left = shift(add(parts[2], right), 1), shift(add(parts[-3], left), -1)
    right, left = shift(add(parts[1], right), 1), shift(add(parts[-2], left), -1)
    return parts[0], right, shift(add(parts[-1], left), -1)


def requested(lists, me, stored_blocks):
    entry = lax.broadcasted_iota(jnp.int32, lists.shape, 1)
    code = entry * stored_blocks + lists % stored_blocks
    hit = lists // stored_blocks == me
    first = jnp.min(jnp.where(hit, code, 1 << 20), axis=1)
    last = jnp.max(jnp.where(hit, code, -1), axis=1)
    one = jnp.where(last >= 0, first % stored_blocks, -1)
    two = jnp.where(last > first, last % stored_blocks, -1)
    return jnp.stack([one, two], axis=1).reshape(-1)


def local(queries, out_grads, latent, block_lists, block_home):
    ctx_count = lax.axis_size("ctx")
    head_count = lax.axis_size("head")
    me = lax.axis_index("head")
    groups, chosen = block_lists.shape
    tokens, heads, width = queries.shape
    value_width = out_grads.shape[2]
    group_rows = tokens // groups
    stored_blocks = latent.shape[0] // BLK
    entries = groups * chosen
    share = BLK // head_count
    pair = BLK // ctx_count
    span = stored_blocks * pair
    rows = group_rows * heads

    spread_rows = spread(block_lists, block_home, latent.T, pair)
    held = lax.all_to_all(
        spread_rows.reshape(ctx_count, span, 640), "ctx", split_axis=0, concat_axis=0, tiled=True
    )
    query_rows = queries.reshape(groups, rows, width)
    grad_rows = out_grads.reshape(groups, rows, value_width)
    entry_of = plan(block_lists, block_home, ctx_count, stored_blocks)
    held, query_rows, entry_of = lax.optimization_barrier((held, query_rows, entry_of))

    outgoing = choose(
        held.reshape(ctx_count * span, 640), width, ctx_count, groups, chosen, pair
    )
    keys0 = lax.all_to_all(outgoing[0], "ctx", split_axis=0, concat_axis=0, tiled=True)
    outgoing1, keys0 = lax.optimization_barrier((outgoing[1], keys0))
    keys1 = lax.all_to_all(outgoing1, "ctx", split_axis=0, concat_axis=0, tiled=True)

    lists = held[:, ::pair, width : width + entries * pair // span].astype(jnp.int32)
    lists = lists.transpose(0, 2, 1).reshape(ctx_count, entries)
    requests_in = requested(lists, lax.axis_index("ctx"), stored_blocks)

    me_ref = me.astype(jnp.int32).reshape(1)
    query_cols0, *parts0 = group_grads(0, 4, me_ref, keys0, query_rows, grad_rows)
    parts0 = dict(zip(OFFSETS, parts0))
    right, left = ring_start(parts0)
    query_cols1, *parts1 = group_grads(1, 1, me_ref, keys1, query_rows, grad_rows)
    parts1[0], right, left = lax.optimization_barrier((parts1[0], right, left))
    by_group = [ring_end(parts0, right, left), ring_whole(dict(zip(OFFSETS, parts1)))]
    query_cols = jnp.stack([query_cols0, query_cols1])
    query_grads = query_cols.reshape(groups, width, group_rows, heads)
    query_grads = query_grads.transpose(0, 2, 3, 1).reshape(tokens, heads, width)

    returned = lax.all_to_all(
        place(entry_of, by_group, share, pair), "ctx", split_axis=0, concat_axis=0, tiled=True
    )
    total = gather_sum(requests_in, returned, stored_blocks)

    minus1, minus2 = shift(total, 1), shift(total, 2)
    plus1, plus2 = shift(total, -1), shift(total, -2)
    minus3, plus3, minus4 = shift(minus2, 1), shift(plus2, -1), shift(minus2, 2)
    pieces = jnp.stack([total, plus1, plus2, plus3, minus4, minus3, minus2, minus1])
    pieces = jnp.roll(pieces, me, axis=0)
    latent_grads = pieces.transpose(1, 0, 2, 3).reshape(stored_blocks * BLK, width)
    return query_grads, latent_grads.astype(jnp.float32)


def solution(mesh):
    in_specs = (P("ctx", "head", None), P("ctx", "head", None), P("ctx", None), P("ctx", None), P())
    out_specs = (P("ctx", "head", None), P("ctx", None))
    return jax.shard_map(local, mesh=mesh, in_specs=in_specs, out_specs=out_specs, check_vma=False)
```

profile of v0, /device:TPU:2, one launch (start us, length us, event | category | flops | bytes accessed | tf_op | source)
XLA Modules:
  0.0 162.7 jit_solution(6818320702705209746)
XLA Ops:
  0.6 2.7 %spread.1 = bf16[512,640]{1,0:T(8,128)(2,1)} custom-call(s32[2,16]{1,0:T(2,128)} %lists_ref.3, s32[256]{0:T(256)} %home_ref.3, bf16[576,512]{1,0:T(8,128)(2,1)} %bitcast.88), custom_call_target="tpu_custom_call" | custom-call | tf_op jit(solution)/shard_map/spread/pallas_call | solution.py:88
  3.4 7.6 %all-to-all-start = ((bf16[32,16,640]{2,1,0:T(8,128)(2,1)}), bf16[32,16,640]{2,1,0:T(8,128)(2,1)S(1)}, u32[]{:S(2)}, u32[]{:S(2)}) async-start(bf16[32,16,640]{2,1,0:T(8,128)(2,1)} %bitcast.87), calls=%async_computation | async-start | bytes 1310720 | tf_op jit(solution)/shard_map/all_to_all | solution.py:359
  11.0 1.5 plan.1.index_ref
  12.5 3.5 %copy.10 = bf16[128,16,576]{2,1,0:T(8,128)(2,1)} copy(bf16[128,16,576]{0,2,1:T(8,128)(2,1)S(1)} %copy-done.3) | data formatting | bytes 4718592 | tf_op args[0]
  16.0 6.8 %all-to-all-done = bf16[32,16,640]{2,1,0:T(8,128)(2,1)S(1)} async-done(((bf16[32,16,640]{2,1,0:T(8,128)(2,1)}), bf16[32,16,640]{2,1,0:T(8,128)(2,1)S(1)}, u32[]{:S(2)}, u32[]{:S(2)}) %all-to-all-start) | async-done | bytes 655392 | tf_op jit(solution)/shard_map/all_to_all | solution.py:359
  22.9 2.9 %choose.1 = (bf16[32,32,576]{2,1,0:T(8,128)(2,1)S(1)}, bf16[32,32,576]{2,1,0:T(8,128)(2,1)}) custom-call(bf16[512,640]{1,0:T(8,128)(2,1)S(1)} %bitcast.80), custom_call_target="tpu_custom_call" | custom-call | tf_op jit(solution)/shard_map/choose/pallas_call | solution.py:118
  25.8 23.9 %all_to_all.20.key_ref = bf16[32,32,576]{2,1,0:T(8,128)(2,1)} all-to-all(bf16[32,32,576]{2,1,0:T(8,128)(2,1)S(1)} %get-tuple-element.32), channel_id=1, replica_groups=mesh['ctx'=32,'head'=8] {'ctx'}, dimensions={0} | all-to-all | bytes 2359296 | tf_op jit(solution)/shard_map/all_to_all | solution.py:370
  49.7 5.1 %all-to-all-start.2 = ((bf16[32,32,576]{2,1,0:T(8,128)(2,1)}), bf16[32,32,576]{2,1,0:T(8,128)(2,1)S(1)}, u32[]{:S(2)}, u32[]{:S(2)}) async-start(bf16[32,32,576]{2,1,0:T(8,128)(2,1)} %get-tuple-element.36), calls=%async_computation.2 | async-start | bytes 2621440 | tf_op jit(solution)/shard_map/all_to_all | solution.py:372
  54.8 15.8 %group_grads.2 = (bf16[576,1024]{1,0:T(8,128)(2,1)}, f32[128,576]{1,0:T(8,128)}, bf16[128,576]{1,0:T(8,128)(2,1)}, bf16[128,576]{1,0:T(8,128)(2,1)}, bf16[128,57...) custom-call(s32[1]{0:T(128)} %bitcast.me_ref, ...), custom_call_target="tpu_custom_call" | custom-call | flops 5771362304 | bytes 8000000 | tf_op jit(solution)/shard_map/group_grads/pallas_call | solution.py:282
  70.6 1.9 %collective-permute-start = (bf16[128,576]{1,0:T(8,128)(2,1)}, bf16[128,576]{1,0:T(8,128)(2,1)S(1)}, u32[]{:S(2)}, u32[]{:S(2)}) collective-permute-start(bf16[128,576]{1,0:T(8,128)(2,1)} %get-tuple-element.44), channel_id=1, source_target_pairs={{0,1},{1,2},{2,3},{3,4},{4,5},{5,6},{6,7},{7,0},{8,9},{9,10},{10,1... | collective-permute-start | bytes 442376 | tf_op jit(solution)/shard_map/ppermute | solution.py:308
  72.5 4.2 %collective-permute-start.1 = (bf16[128,576]{1,0:T(8,128)(2,1)}, bf16[128,576]{1,0:T(8,128)(2,1)S(1)}, u32[]{:S(2)}, u32[]{:S(2)}) collective-permute-start(bf16[128,576]{1,0:T(8,128)(2,1)} %get-tuple-element.45), channel_id=1, source_target_pairs={{0,7},{1,0},{2,1},{3,2},{4,3},{5,4},{6,5},{7,6},{8,15},{9,8},{10,9... | collective-permute-start | bytes 442376 | tf_op jit(solution)/shard_map/ppermute | solution.py:308
  76.7 1.1 copy-done.4
  77.8 11.2 %group_grads.3 = (bf16[576,1024]{1,0:T(8,128)(2,1)}, f32[128,576]{1,0:T(8,128)}, bf16[128,576]{1,0:T(8,128)(2,1)}, bf16[128,576]{1,0:T(8,128)(2,1)}, bf16[128,57...) custom-call(s32[1]{0:T(128)} %bitcast.me_ref, ...), custom_call_target="tpu_custom_call" | custom-call | flops 5771362304 | bytes 8000000 | tf_op jit(solution)/shard_map/group_grads/pallas_call | solution.py:282
  89.1 3.2 %collective-permute-start.10 = (bf16[128,576]{1,0:T(8,128)(2,1)}, bf16[128,576]{1,0:T(8,128)(2,1)S(1)}, u32[]{:S(2)}, u32[]{:S(2)}) collective-permute-start(bf16[128,576]{1,0:T(8,128)(2,1)} %get-tuple-element.57), channel_id=1, source_target_pairs={{0,7},{1,0},{2,1},{3,2},{4,3},{5,4},{6,5},{7,6},{8,15},{9,8},{10,9... | collective-permute-start | bytes 442376 | tf_op jit(solution)/shard_map/ppermute | solution.py:308
  92.4 1.8 %collective-permute-start.5 = (bf16[128,576]{1,0:T(8,128)(2,1)S(1)}, bf16[128,576]{1,0:T(8,128)(2,1)S(1)}, u32[]{:S(2)}, u32[]{:S(2)}) collective-permute-start(bf16[128,576]{1,0:T(8,128)(2,1)S(1)} %add_convert_fusion.6), channel_id=1, source_target_pairs={{0,7},{1,0},{2,1},{3,2},{4,3},{5,4},{6,5},{7,6},{8,15},{9,8},{10,9... | collective-permute-start | bytes 442376 | tf_op jit(solution)/shard_map/ppermute | solution.py:308
  94.3 0.4 collective-permute-start.2
  94.6 2.1 %collective-permute-done.7 = bf16[128,576]{1,0:T(8,128)(2,1)S(1)} collective-permute-done((bf16[128,576]{1,0:T(8,128)(2,1)}, bf16[128,576]{1,0:T(8,128)(2,1)S(1)}, u32[]{:S(2)}, u32[]{:S(2)}) %collective-permute-start.7) | collective-permute-done | bytes 147488 | tf_op jit(solution)/shard_map/ppermute | solution.py:308
  96.7 1.0 add_convert_fusion.4
  97.8 3.3 %collective-permute-start.11 = (bf16[128,576]{1,0:T(8,128)(2,1)S(1)}, bf16[128,576]{1,0:T(8,128)(2,1)S(1)}, u32[]{:S(2)}, u32[]{:S(2)}) collective-permute-start(bf16[128,576]{1,0:T(8,128)(2,1)S(1)} %add_convert_fusion.2), channel_id=1, source_target_pairs={{0,7},{1,0},{2,1},{3,2},{4,3},{5,4},{6,5},{7,6},{8,15},{9,8},{10,9... | collective-permute-start | bytes 442376 | tf_op jit(solution)/shard_map/ppermute | solution.py:308
  101.2 2.2 %collective-permute-start.6 = (bf16[128,576]{1,0:T(8,128)(2,1)S(1)}, bf16[128,576]{1,0:T(8,128)(2,1)S(1)}, u32[]{:S(2)}, u32[]{:S(2)}) collective-permute-start(bf16[128,576]{1,0:T(8,128)(2,1)S(1)} %add_convert_fusion.5), channel_id=1, source_target_pairs={{0,7},{1,0},{2,1},{3,2},{4,3},{5,4},{6,5},{7,6},{8,15},{9,8},{10,9... | collective-permute-start | bytes 442376 | tf_op jit(solution)/shard_map/ppermute | solution.py:308
  103.4 0.3 collective-permute-start.3
  103.8 0.7 collective-permute-done.8
  104.6 0.9 collective-permute-done.11
  105.5 3.8 %collective-permute-start.12 = (bf16[128,576]{1,0:T(8,128)(2,1)S(1)}, bf16[128,576]{1,0:T(8,128)(2,1)S(1)}, u32[]{:S(2)}, u32[]{:S(2)}) collective-permute-start(bf16[128,576]{1,0:T(8,128)(2,1)S(1)} %add_convert_fusion.1), channel_id=1, source_target_pairs={{0,7},{1,0},{2,1},{3,2},{4,3},{5,4},{6,5},{7,6},{8,15},{9,8},{10,9... | collective-permute-start | bytes 442376 | tf_op jit(solution)/shard_map/ppermute | solution.py:308
  109.2 2.3 %collective-permute-done.3 = bf16[128,576]{1,0:T(8,128)(2,1)S(1)} collective-permute-done((bf16[128,576]{1,0:T(8,128)(2,1)S(1)}, bf16[128,576]{1,0:T(8,128)(2,1)S(1)}, u32[]{:S(2)}, u32[]{:S(2)}) %collective-permute-start.3) | collective-permute-done | bytes 147488 | tf_op jit(solution)/shard_map/ppermute | solution.py:308
  111.7 0.4 collective-permute-done.12
  112.1 3.8 %collective-permute-start.13 = (bf16[128,576]{1,0:T(8,128)(2,1)S(1)}, bf16[128,576]{1,0:T(8,128)(2,1)S(1)}, u32[]{:S(2)}, u32[]{:S(2)}) collective-permute-start(bf16[128,576]{1,0:T(8,128)(2,1)S(1)} %add_convert_fusion), channel_id=1, source_target_pairs={{0,7},{1,0},{2,1},{3,2},{4,3},{5,4},{6,5},{7,6},{8,15},{9,8},{10,9... | collective-permute-start | bytes 442376 | tf_op jit(solution)/shard_map/ppermute | solution.py:308
  115.9 0.3 slice.3
  116.2 2.0 %collective-permute-done.4.refs_1_ = bf16[128,576]{1,0:T(8,128)(2,1)S(1)} collective-permute-done((bf16[128,576]{1,0:T(8,128)(2,1)S(1)}, bf16[128,576]{1,0:T(8,128)(2,1)S(1)}, u32[]{:S(2)}, u32[]{:S(2)}) %collective-permute-start.4) | collective-permute-done | bytes 147488 | tf_op jit(solution)/shard_map/ppermute | solution.py:308
  118.2 0.5 collective-permute-done.13.refs_5_
  118.7 2.4 %place.1 = bf16[64,8,576]{2,1,0:T(8,128)(2,1)} custom-call(s32[64]{0:T(128)S(1)} %copy-done.2, f32[128,576]{1,0:T(8,128)S(1)} %copy-done, bf16[128,576]{1,0:T(8,128)(2,1)S(1)} %collective-permute-done.4.refs_1_, bf16[128,576]{1,0:T(8,128)(2,1)S(1)} %collective-permute-done.6.refs_2_, f32[128,576]{1,0:T(8,128)S(1)} %copy-done.1, ...), custom_call_target="tpu_custom_call" | custom-call | tf_op jit(solution)/shard_map/place/pallas_call | solution.py:163
  121.1 7.5 %all-to-all-start.3 = ((bf16[64,8,576]{2,1,0:T(8,128)(2,1)}), bf16[64,8,576]{2,1,0:T(8,128)(2,1)S(1)}, u32[]{:S(2)}, u32[]{:S(2)}) async-start(bf16[64,8,576]{2,1,0:T(8,128)(2,1)} %place.1), calls=%async_computation.3 | async-start | bytes 1310720 | tf_op jit(solution)/shard_map/all_to_all | solution.py:389
  128.7 1.3 select_reduce_fusion.1
  130.0 0.1 reshape.143.index_ref
  130.2 1.5 copy.11
  131.7 1.4 copy.12
  133.1 2.1 %pad_maximum_fusion = bf16[2,576,64,16]{1,3,2,0:T(8,128)(2,1)S(1)} fusion(bf16[1,576,64,16]{1,3,2,0:T(8,128)(2,1)} %bitcast.83, bf16[1,576,64,16]{1,3,2,0:T(8,128)(2,1)} %bitcast.82), kind=kLoop, calls=%fused_computation | loop fusion | flops 1179648 | bytes 4718592 | tf_op jit(solution)/shard_map/stack | solution.py:385
  135.2 3.1 %copy.15 = bf16[128,16,576]{0,2,1:T(8,128)(2,1)} copy(bf16[128,16,576]{2,1,0:T(8,128)(2,1)S(1)} %bitcast.81) | data formatting | bytes 4718592
  138.3 2.3 %all-to-all-done.3.rows_ref = bf16[64,8,576]{2,1,0:T(8,128)(2,1)S(1)} async-done(((bf16[64,8,576]{2,1,0:T(8,128)(2,1)}), bf16[64,8,576]{2,1,0:T(8,128)(2,1)S(1)}, u32[]{:S(2)}, u32[]{:S(2)}) %all-to-all-start.3) | async-done | bytes 589856 | tf_op jit(solution)/shard_map/all_to_all | solution.py:389
  140.6 0.9 gather_sum.1
  141.6 6.0 %collective-permute-start.17 = (bf16[8,8,576]{2,1,0:T(8,128)(2,1)S(1)}, bf16[8,8,576]{2,1,0:T(8,128)(2,1)S(1)}, u32[]{:S(2)}, u32[]{:S(2)}) collective-permute-start(bf16[8,8,576]{2,1,0:T(8,128)(2,1)S(1)} %gather_sum.1), channel_id=1, source_target_pairs={{0,2},{1,3},{2,4},{3,5},{4,6},{5,7},{6,0},{7,1},{8,10},{9,11},{10,... | collective-permute-start | bytes 221192 | tf_op jit(solution)/shard_map/ppermute | solution.py:308
  147.6 0.7 collective-permute-start.14
  148.3 4.9 %collective-permute-done.17 = bf16[8,8,576]{2,1,0:T(8,128)(2,1)S(1)} collective-permute-done((bf16[8,8,576]{2,1,0:T(8,128)(2,1)S(1)}, bf16[8,8,576]{2,1,0:T(8,128)(2,1)S(1)}, u32[]{:S(2)}, u32[]{:S(2)}) %collective-permute-start.17) | collective-permute-done | bytes 73760 | tf_op jit(solution)/shard_map/ppermute | solution.py:308
  153.2 0.9 collective-permute-start.18
  154.1 0.2 collective-permute-done.15
  154.3 3.0 %collective-permute-start.16 = (bf16[8,8,576]{2,1,0:T(8,128)(2,1)S(1)}, bf16[8,8,576]{2,1,0:T(8,128)(2,1)S(1)}, u32[]{:S(2)}, u32[]{:S(2)}) collective-permute-start(bf16[8,8,576]{2,1,0:T(8,128)(2,1)S(1)} %collective-permute-done.15), channel_id=1, source_target_pairs={{0,7},{1,0},{2,1},{3,2},{4,3},{5,4},{6,5},{7,6},{8,15},{9,8},{10,9... | collective-permute-start | bytes 221192 | tf_op jit(solution)/shard_map/ppermute | solution.py:308
  157.3 3.5 %collective-permute-done.16 = bf16[8,8,576]{2,1,0:T(8,128)(2,1)S(1)} collective-permute-done((bf16[8,8,576]{2,1,0:T(8,128)(2,1)S(1)}, bf16[8,8,576]{2,1,0:T(8,128)(2,1)S(1)}, u32[]{:S(2)}, u32[]{:S(2)}) %collective-permute-start.16) | collective-permute-done | bytes 73760 | tf_op jit(solution)/shard_map/ppermute | solution.py:308
  161.3 1.4 copy.16
  (81 shorter events, 1.4 us)
Async XLA Ops:
  0.6 11.9 %copy-start.3 = (bf16[128,16,576]{0,2,1:T(8,128)(2,1)S(1)}, bf16[128,16,576]{0,2,1:T(8,128)(2,1)}, u32[]{:S(2)}) copy-start(bf16[128,16,576]{0,2,1:T(8,128)(2,1)} %param.5) | copy-start | bytes 7077892
  3.4 19.5 %all-to-all-start = ((bf16[32,16,640]{2,1,0:T(8,128)(2,1)}), bf16[32,16,640]{2,1,0:T(8,128)(2,1)S(1)}, u32[]{:S(2)}, u32[]{:S(2)}) async-start(bf16[32,16,640]{2,1,0:T(8,128)(2,1)} %bitcast.87), calls=%async_computation | async-start | bytes 1310720 | tf_op jit(solution)/shard_map/all_to_all | solution.py:359
  49.7 27.0 %all-to-all-start.2 = ((bf16[32,32,576]{2,1,0:T(8,128)(2,1)}), bf16[32,32,576]{2,1,0:T(8,128)(2,1)S(1)}, u32[]{:S(2)}, u32[]{:S(2)}) async-start(bf16[32,32,576]{2,1,0:T(8,128)(2,1)} %get-tuple-element.36), calls=%async_computation.2 | async-start | bytes 2621440 | tf_op jit(solution)/shard_map/all_to_all | solution.py:372
  70.6 21.7 %collective-permute-start = (bf16[128,576]{1,0:T(8,128)(2,1)}, bf16[128,576]{1,0:T(8,128)(2,1)S(1)}, u32[]{:S(2)}, u32[]{:S(2)}) collective-permute-start(bf16[128,576]{1,0:T(8,128)(2,1)} %get-tuple-element.44), channel_id=1, source_target_pairs={{0,1},{1,2},{2,3},{3,4},{4,5},{5,6},{6,7},{7,0},{8,9},{9,10},{10,1... | collective-permute-start | bytes 442376 | tf_op jit(solution)/shard_map/ppermute | solution.py:308
  72.5 19.8 %copy-start.15 = (bf16[128,576]{1,0:T(8,128)(2,1)S(1)}, bf16[128,576]{1,0:T(8,128)(2,1)}, u32[]{:S(2)}) copy-start(bf16[128,576]{1,0:T(8,128)(2,1)} %get-tuple-element.48) | copy-start | bytes 442372
  72.5 21.7 %copy-start.13 = (bf16[128,576]{1,0:T(8,128)(2,1)S(1)}, bf16[128,576]{1,0:T(8,128)(2,1)}, u32[]{:S(2)}) copy-start(bf16[128,576]{1,0:T(8,128)(2,1)} %get-tuple-element.42) | copy-start | bytes 442372
  72.5 19.8 %collective-permute-start.1 = (bf16[128,576]{1,0:T(8,128)(2,1)}, bf16[128,576]{1,0:T(8,128)(2,1)S(1)}, u32[]{:S(2)}, u32[]{:S(2)}) collective-permute-start(bf16[128,576]{1,0:T(8,128)(2,1)} %get-tuple-element.45), channel_id=1, source_target_pairs={{0,7},{1,0},{2,1},{3,2},{4,3},{5,4},{6,5},{7,6},{8,15},{9,8},{10,9... | collective-permute-start | bytes 442376 | tf_op jit(solution)/shard_map/ppermute | solution.py:308
  76.7 1.1 copy-start.4
  89.0 8.8 %copy-start.14 = (bf16[128,576]{1,0:T(8,128)(2,1)S(1)}, bf16[128,576]{1,0:T(8,128)(2,1)}, u32[]{:S(2)}) copy-start(bf16[128,576]{1,0:T(8,128)(2,1)} %get-tuple-element.56) | copy-start | bytes 442372
  89.0 12.1 %copy-start.11 = (bf16[128,576]{1,0:T(8,128)(2,1)S(1)}, bf16[128,576]{1,0:T(8,128)(2,1)}, u32[]{:S(2)}) copy-start(bf16[128,576]{1,0:T(8,128)(2,1)} %get-tuple-element.47) | copy-start | bytes 442372
  89.0 14.4 %copy-start.9 = (bf16[128,576]{1,0:T(8,128)(2,1)S(1)}, bf16[128,576]{1,0:T(8,128)(2,1)}, u32[]{:S(2)}) copy-start(bf16[128,576]{1,0:T(8,128)(2,1)} %get-tuple-element.41) | copy-start | bytes 442372
  89.0 7.7 %collective-permute-start.7 = (bf16[128,576]{1,0:T(8,128)(2,1)}, bf16[128,576]{1,0:T(8,128)(2,1)S(1)}, u32[]{:S(2)}, u32[]{:S(2)}) collective-permute-start(bf16[128,576]{1,0:T(8,128)(2,1)} %get-tuple-element.53), channel_id=1, source_target_pairs={{0,1},{1,2},{2,3},{3,4},{4,5},{5,6},{6,7},{7,0},{8,9},{9,10},{10,1... | collective-permute-start | bytes 442376 | tf_op jit(solution)/shard_map/ppermute | solution.py:308
  89.1 8.7 %collective-permute-start.10 = (bf16[128,576]{1,0:T(8,128)(2,1)}, bf16[128,576]{1,0:T(8,128)(2,1)S(1)}, u32[]{:S(2)}, u32[]{:S(2)}) collective-permute-start(bf16[128,576]{1,0:T(8,128)(2,1)} %get-tuple-element.57), channel_id=1, source_target_pairs={{0,7},{1,0},{2,1},{3,2},{4,3},{5,4},{6,5},{7,6},{8,15},{9,8},{10,9... | collective-permute-start | bytes 442376 | tf_op jit(solution)/shard_map/ppermute | solution.py:308
  92.4 12.0 %copy-start.12 = (bf16[128,576]{1,0:T(8,128)(2,1)S(1)}, bf16[128,576]{1,0:T(8,128)(2,1)}, u32[]{:S(2)}) copy-start(bf16[128,576]{1,0:T(8,128)(2,1)} %get-tuple-element.51) | copy-start | bytes 442372
  92.4 8.7 %collective-permute-start.5 = (bf16[128,576]{1,0:T(8,128)(2,1)S(1)}, bf16[128,576]{1,0:T(8,128)(2,1)S(1)}, u32[]{:S(2)}, u32[]{:S(2)}) collective-permute-start(bf16[128,576]{1,0:T(8,128)(2,1)S(1)} %add_convert_fusion.6), channel_id=1, source_target_pairs={{0,7},{1,0},{2,1},{3,2},{4,3},{5,4},{6,5},{7,6},{8,15},{9,8},{10,9... | collective-permute-start | bytes 442376 | tf_op jit(solution)/shard_map/ppermute | solution.py:308
  94.2 11.2 %copy-start.10 = (bf16[128,576]{1,0:T(8,128)(2,1)S(1)}, bf16[128,576]{1,0:T(8,128)(2,1)}, u32[]{:S(2)}) copy-start(bf16[128,576]{1,0:T(8,128)(2,1)} %get-tuple-element.55) | copy-start | bytes 442372
  94.3 9.1 %collective-permute-start.2 = (bf16[128,576]{1,0:T(8,128)(2,1)S(1)}, bf16[128,576]{1,0:T(8,128)(2,1)S(1)}, u32[]{:S(2)}, u32[]{:S(2)}) collective-permute-start(bf16[128,576]{1,0:T(8,128)(2,1)S(1)} %add_convert_fusion.9), channel_id=1, source_target_pairs={{0,1},{1,2},{2,3},{3,4},{4,5},{5,6},{6,7},{7,0},{8,9},{9,10},{10,1... | collective-permute-start | bytes 442376 | tf_op jit(solution)/shard_map/ppermute | solution.py:308
  97.7 13.9 %copy-start.7 = (bf16[128,576]{1,0:T(8,128)(2,1)S(1)}, bf16[128,576]{1,0:T(8,128)(2,1)}, u32[]{:S(2)}) copy-start(bf16[128,576]{1,0:T(8,128)(2,1)} %get-tuple-element.40) | copy-start | bytes 442372
  97.7 6.8 %collective-permute-start.8 = (bf16[128,576]{1,0:T(8,128)(2,1)S(1)}, bf16[128,576]{1,0:T(8,128)(2,1)S(1)}, u32[]{:S(2)}, u32[]{:S(2)}) collective-permute-start(bf16[128,576]{1,0:T(8,128)(2,1)S(1)} %add_convert_fusion.4), channel_id=1, source_target_pairs={{0,1},{1,2},{2,3},{3,4},{4,5},{5,6},{6,7},{7,0},{8,9},{9,10},{10,1... | collective-permute-start | bytes 442376 | tf_op jit(solution)/shard_map/ppermute | solution.py:308
  97.8 14.2 %copy-start.8 = (bf16[128,576]{1,0:T(8,128)(2,1)S(1)}, bf16[128,576]{1,0:T(8,128)(2,1)}, u32[]{:S(2)}) copy-start(bf16[128,576]{1,0:T(8,128)(2,1)} %get-tuple-element.54) | copy-start | bytes 442372
  97.8 7.6 %collective-permute-start.11 = (bf16[128,576]{1,0:T(8,128)(2,1)S(1)}, bf16[128,576]{1,0:T(8,128)(2,1)S(1)}, u32[]{:S(2)}, u32[]{:S(2)}) collective-permute-start(bf16[128,576]{1,0:T(8,128)(2,1)S(1)} %add_convert_fusion.2), channel_id=1, source_target_pairs={{0,7},{1,0},{2,1},{3,2},{4,3},{5,4},{6,5},{7,6},{8,15},{9,8},{10,9... | collective-permute-start | bytes 442376 | tf_op jit(solution)/shard_map/ppermute | solution.py:308
  101.2 15.0 %collective-permute-start.6 = (bf16[128,576]{1,0:T(8,128)(2,1)S(1)}, bf16[128,576]{1,0:T(8,128)(2,1)S(1)}, u32[]{:S(2)}, u32[]{:S(2)}) collective-permute-start(bf16[128,576]{1,0:T(8,128)(2,1)S(1)} %add_convert_fusion.5), channel_id=1, source_target_pairs={{0,7},{1,0},{2,1},{3,2},{4,3},{5,4},{6,5},{7,6},{8,15},{9,8},{10,9... | collective-permute-start | bytes 442376 | tf_op jit(solution)/shard_map/ppermute | solution.py:308
  103.4 15.4 %copy-start = (f32[128,576]{1,0:T(8,128)S(1)}, f32[128,576]{1,0:T(8,128)}, u32[]{:S(2)}) copy-start(f32[128,576]{1,0:T(8,128)} %get-tuple-element.39.refs_0_) | copy-start | bytes 884740
  103.4 15.4 %copy-start.1 = (f32[128,576]{1,0:T(8,128)S(1)}, f32[128,576]{1,0:T(8,128)}, u32[]{:S(2)}) copy-start(f32[128,576]{1,0:T(8,128)} %get-tuple-element.50.refs_3_) | copy-start | bytes 884740
  103.4 15.3 %copy-start.2 = (s32[64]{0:T(128)S(1)}, s32[64]{0:T(128)}, u32[]{:S(2)}) copy-start(s32[64]{0:T(128)} %plan.1.index_ref) | copy-start | bytes 772
  103.4 8.1 %collective-permute-start.3 = (bf16[128,576]{1,0:T(8,128)(2,1)S(1)}, bf16[128,576]{1,0:T(8,128)(2,1)S(1)}, u32[]{:S(2)}, u32[]{:S(2)}) collective-permute-start(bf16[128,576]{1,0:T(8,128)(2,1)S(1)} %add_convert_fusion.8), channel_id=1, source_target_pairs={{0,1},{1,2},{2,3},{3,4},{4,5},{5,6},{6,7},{7,0},{8,9},{9,10},{10,1... | collective-permute-start | bytes 442376 | tf_op jit(solution)/shard_map/ppermute | solution.py:308
  104.5 11.7 %collective-permute-start.9 = (bf16[128,576]{1,0:T(8,128)(2,1)S(1)}, bf16[128,576]{1,0:T(8,128)(2,1)S(1)}, u32[]{:S(2)}, u32[]{:S(2)}) collective-permute-start(bf16[128,576]{1,0:T(8,128)(2,1)S(1)} %add_convert_fusion.3), channel_id=1, source_target_pairs={{0,1},{1,2},{2,3},{3,4},{4,5},{5,6},{6,7},{7,0},{8,9},{9,10},{10,1... | collective-permute-start | bytes 442376 | tf_op jit(solution)/shard_map/ppermute | solution.py:308
  105.5 6.6 %collective-permute-start.12 = (bf16[128,576]{1,0:T(8,128)(2,1)S(1)}, bf16[128,576]{1,0:T(8,128)(2,1)S(1)}, u32[]{:S(2)}, u32[]{:S(2)}) collective-permute-start(bf16[128,576]{1,0:T(8,128)(2,1)S(1)} %add_convert_fusion.1), channel_id=1, source_target_pairs={{0,7},{1,0},{2,1},{3,2},{4,3},{5,4},{6,5},{7,6},{8,15},{9,8},{10,9... | collective-permute-start | bytes 442376 | tf_op jit(solution)/shard_map/ppermute | solution.py:308
  111.6 6.6 %collective-permute-start.4 = (bf16[128,576]{1,0:T(8,128)(2,1)S(1)}, bf16[128,576]{1,0:T(8,128)(2,1)S(1)}, u32[]{:S(2)}, u32[]{:S(2)}) collective-permute-start(bf16[128,576]{1,0:T(8,128)(2,1)S(1)} %add_convert_fusion.7), channel_id=1, source_target_pairs={{0,1},{1,2},{2,3},{3,4},{4,5},{5,6},{6,7},{7,0},{8,9},{9,10},{10,1... | collective-permute-start | bytes 442376 | tf_op jit(solution)/shard_map/ppermute | solution.py:308
  112.1 6.6 %collective-permute-start.13 = (bf16[128,576]{1,0:T(8,128)(2,1)S(1)}, bf16[128,576]{1,0:T(8,128)(2,1)S(1)}, u32[]{:S(2)}, u32[]{:S(2)}) collective-permute-start(bf16[128,576]{1,0:T(8,128)(2,1)S(1)} %add_convert_fusion), channel_id=1, source_target_pairs={{0,7},{1,0},{2,1},{3,2},{4,3},{5,4},{6,5},{7,6},{8,15},{9,8},{10,9... | collective-permute-start | bytes 442376 | tf_op jit(solution)/shard_map/ppermute | solution.py:308
  118.7 11.4 %copy-start.5 = (bf16[576,1024]{1,0:T(8,128)(2,1)S(1)}, bf16[576,1024]{1,0:T(8,128)(2,1)}, u32[]{:S(2)}) copy-start(bf16[576,1024]{1,0:T(8,128)(2,1)} %get-tuple-element.35) | copy-start | bytes 3538948
  121.1 19.4 %all-to-all-start.3 = ((bf16[64,8,576]{2,1,0:T(8,128)(2,1)}), bf16[64,8,576]{2,1,0:T(8,128)(2,1)S(1)}, u32[]{:S(2)}, u32[]{:S(2)}) async-start(bf16[64,8,576]{2,1,0:T(8,128)(2,1)} %place.1), calls=%async_computation.3 | async-start | bytes 1310720 | tf_op jit(solution)/shard_map/all_to_all | solution.py:389
  128.7 3.0 %copy-start.6 = (bf16[576,1024]{1,0:T(8,128)(2,1)S(1)}, bf16[576,1024]{1,0:T(8,128)(2,1)}, u32[]{:S(2)}) copy-start(bf16[576,1024]{1,0:T(8,128)(2,1)} %get-tuple-element.37) | copy-start | bytes 3538948
  141.5 19.5 %collective-permute-start.20 = (bf16[8,8,576]{2,1,0:T(8,128)(2,1)S(1)}, bf16[8,8,576]{2,1,0:T(8,128)(2,1)S(1)}, u32[]{:S(2)}, u32[]{:S(2)}) collective-permute-start(bf16[8,8,576]{2,1,0:T(8,128)(2,1)S(1)} %gather_sum.1), channel_id=1, source_target_pairs={{0,1},{1,2},{2,3},{3,4},{4,5},{5,6},{6,7},{7,0},{8,9},{9,10},{10,1... | collective-permute-start | bytes 221192 | tf_op jit(solution)/shard_map/ppermute | solution.py:308
  141.6 11.6 %collective-permute-start.17 = (bf16[8,8,576]{2,1,0:T(8,128)(2,1)S(1)}, bf16[8,8,576]{2,1,0:T(8,128)(2,1)S(1)}, u32[]{:S(2)}, u32[]{:S(2)}) collective-permute-start(bf16[8,8,576]{2,1,0:T(8,128)(2,1)S(1)} %gather_sum.1), channel_id=1, source_target_pairs={{0,2},{1,3},{2,4},{3,5},{4,6},{5,7},{6,0},{7,1},{8,10},{9,11},{10,... | collective-permute-start | bytes 221192 | tf_op jit(solution)/shard_map/ppermute | solution.py:308
  147.6 6.7 %collective-permute-start.15 = (bf16[8,8,576]{2,1,0:T(8,128)(2,1)S(1)}, bf16[8,8,576]{2,1,0:T(8,128)(2,1)S(1)}, u32[]{:S(2)}, u32[]{:S(2)}) collective-permute-start(bf16[8,8,576]{2,1,0:T(8,128)(2,1)S(1)} %gather_sum.1), channel_id=1, source_target_pairs={{0,6},{1,7},{2,0},{3,1},{4,2},{5,3},{6,4},{7,5},{8,14},{9,15},{10,... | collective-permute-start | bytes 221192 | tf_op jit(solution)/shard_map/ppermute | solution.py:308
  147.6 9.7 %collective-permute-start.14 = (bf16[8,8,576]{2,1,0:T(8,128)(2,1)S(1)}, bf16[8,8,576]{2,1,0:T(8,128)(2,1)S(1)}, u32[]{:S(2)}, u32[]{:S(2)}) collective-permute-start(bf16[8,8,576]{2,1,0:T(8,128)(2,1)S(1)} %gather_sum.1), channel_id=1, source_target_pairs={{0,7},{1,0},{2,1},{3,2},{4,3},{5,4},{6,5},{7,6},{8,15},{9,8},{10,9... | collective-permute-start | bytes 221192 | tf_op jit(solution)/shard_map/ppermute | solution.py:308
  153.1 7.7 %collective-permute-start.19 = (bf16[8,8,576]{2,1,0:T(8,128)(2,1)S(1)}, bf16[8,8,576]{2,1,0:T(8,128)(2,1)S(1)}, u32[]{:S(2)}, u32[]{:S(2)}) collective-permute-start(bf16[8,8,576]{2,1,0:T(8,128)(2,1)S(1)} %collective-permute-done.17), channel_id=1, source_target_pairs={{0,1},{1,2},{2,3},{3,4},{4,5},{5,6},{6,7},{7,0},{8,9},{9,10},{10,1... | collective-permute-start | bytes 221192 | tf_op jit(solution)/shard_map/ppermute | solution.py:308
  153.2 7.7 %collective-permute-start.18 = (bf16[8,8,576]{2,1,0:T(8,128)(2,1)S(1)}, bf16[8,8,576]{2,1,0:T(8,128)(2,1)S(1)}, u32[]{:S(2)}, u32[]{:S(2)}) collective-permute-start(bf16[8,8,576]{2,1,0:T(8,128)(2,1)S(1)} %collective-permute-done.17), channel_id=1, source_target_pairs={{0,2},{1,3},{2,4},{3,5},{4,6},{5,7},{6,0},{7,1},{8,10},{9,11},{10,... | collective-permute-start | bytes 221192 | tf_op jit(solution)/shard_map/ppermute | solution.py:308
  154.3 6.6 %collective-permute-start.16 = (bf16[8,8,576]{2,1,0:T(8,128)(2,1)S(1)}, bf16[8,8,576]{2,1,0:T(8,128)(2,1)S(1)}, u32[]{:S(2)}, u32[]{:S(2)}) collective-permute-start(bf16[8,8,576]{2,1,0:T(8,128)(2,1)S(1)} %collective-permute-done.15), channel_id=1, source_target_pairs={{0,7},{1,0},{2,1},{3,2},{4,3},{5,4},{6,5},{7,6},{8,15},{9,8},{10,9... | collective-permute-start | bytes 221192 | tf_op jit(solution)/shard_map/ppermute | solution.py:308
where the time goes:
time: 164 us; the launch traced here: 163 us
  starting transfers between devices  56.1 us (34%)
  Pallas kernels  37.4 us (23%)
  waiting for transfers between devices  26.6 us (16%)
  blocking collectives  23.9 us (15%)
  local copies, waits for them, and re-layouts  12.9 us (8%)
  other arithmetic  4.83 us (3%)
    ppermute x21, starting transfers between devices, shift(): lax.ppermute(x, 'head', [(i, (i + by) % count) for i in range(count)])  35.9 us
    pallas_call x2, Pallas kernels, group_grads(): pl.pallas_call(functools.partial(group_kernel, pieces), grid=(1,), in_spe...  27 us
    all_to_all x1, blocking collectives, local(): lax.all_to_all(outgoing[0], 'ctx', split_axis=0, concat_axis=0, tiled=True)  23.9 us
    ppermute x21, waiting for transfers between devices, shift(): lax.ppermute(x, 'head', [(i, (i + by) % count) for i in range(count)])  17.4 us
    unnamed x50, local copies, waits for them, and re-layouts  9.39 us
    all_to_all x1, starting transfers between devices, local(): lax.all_to_all(spread_rows.reshape(ctx_count, span, 640), 'ctx', split_ax...  7.62 us
    all_to_all x1, starting transfers between devices, local(): lax.all_to_all(place(entry_of, by_group, share, pair), 'ctx', split_axis=...  7.52 us
    all_to_all x1, waiting for transfers between devices, local(): lax.all_to_all(spread_rows.reshape(ctx_count, span, 640), 'ctx', split_ax...  6.84 us
  transfers between devices with their start and end apart: 24, of which 12 were waited for; matrix products, arithmetic and copies ran while one was open for 9% of the time, Pallas kernels for 18%

commit v1 on v0

--- a/solution.py
+++ b/solution.py
@@ -12,6 +12,7 @@
 LOG2E = 1.4426950408889634
 softmax_scale = 192.0 ** (-0.5)
 LARGE_LIMIT = 56 * 1024 * 1024
+GROUP_LIMITS = (56 * 1024 * 1024, 50 * 1024 * 1024)
 SMALL_LIMIT = 16 * 1024 * 1024
 ROWS_BY_ROWS = (((1,), (1,)), ((), ()))
 COLS_BY_COLS = (((0,), (0,)), ((), ()))
@@ -59,7 +60,7 @@
     width, tokens = latent_ref.shape
     stored = tokens // BLK
     span = stored * pair
-    row = lax.broadcasted_iota(jnp.int32, (tokens, tokens), 0)
+    row = lax.broadcasted_iota(jnp.int32, (tokens, 1), 0)
     col = lax.broadcasted_iota(jnp.int32, (tokens, tokens), 1)
     source = (row % span) // pair * BLK + row // span * pair + row % pair
     moved = lax.dot_general(
@@ -95,32 +96,34 @@
     )(block_lists, block_home, latent_cols)
 
 
-def choose_kernel(pair, held_ref, *out_refs):
-    targets, _, width = out_refs[0].shape
+def choose_kernel(first, pair, held_ref, out_ref):
+    targets, total, width = out_ref.shape
     count = held_ref.shape[0]
     span = count // targets
-    steps = out_refs[0].shape[1] // span
-    rows = held_ref[:, :width]
-    lists = held_ref[:, width:].astype(jnp.float32)
     parity = lax.broadcasted_iota(jnp.int32, (count, 1), 0) % pair
     col = lax.broadcasted_iota(jnp.int32, (count, count), 1).astype(jnp.float32)
-    for group, out_ref in enumerate(out_refs):
-        for step in range(steps):
-            at = group * steps + step
-            source = lists[:, at : at + 1] * pair + parity.astype(jnp.float32)
-            chosen = jnp.dot(one_hot(col == source), rows, preferred_element_type=jnp.float32)
-            chosen = chosen.astype(out_ref.dtype).reshape(targets, span, width)
-            out_ref[:, step * span : (step + 1) * span] = chosen
-
-
-def choose(held, width, targets, groups, chosen, pair):
-    one = jax.ShapeDtypeStruct((targets, chosen * pair, width), held.dtype)
-    return pl.pallas_call(
-        functools.partial(choose_kernel, pair),
-        out_shape=[one] * groups,
+    for step in range(total // span):
+        at = width + first + step
+        positions = held_ref[:, at : at + 1].astype(jnp.float32)
+        source = positions * pair + parity.astype(jnp.float32)
+        chosen = jnp.dot(
+            one_hot(col == source), held_ref[:, :width], preferred_element_type=jnp.float32
+        )
+        chosen = chosen.astype(out_ref.dtype).reshape(targets, span, width)
+        out_ref[:, step * span : (step + 1) * span] = chosen
+
+
+def choose(group, held, width, targets, chosen, pair):
+    span = held.shape[0] // targets
+    return pl.pallas_call(
+        functools.partial(choose_kernel, group * chosen * pair // span, pair),
+        out_shape=jax.ShapeDtypeStruct((targets, chosen * pair, width), held.dtype),
         in_specs=[vmem()],
-        out_specs=[vmem()] * groups,
-        compiler_params=pltpu.CompilerParams(vmem_limit_bytes=SMALL_LIMIT),
+        out_specs=vmem(),
+        compiler_params=pltpu.CompilerParams(vmem_limit_bytes=(SMALL_LIMIT, LARGE_LIMIT)[group]),
+        cost_estimate=pl.CostEstimate(
+            flops=4 * held.shape[0] ** 2 * width, bytes_accessed=2_000_000, transcendentals=0
+        ),
         name="choose",
     )(held)
 
@@ -295,7 +298,7 @@
             pltpu.VMEM((key_count, rows), jnp.bfloat16),
             pltpu.VMEM((key_count, rows), jnp.bfloat16),
         ],
-        compiler_params=pltpu.CompilerParams(vmem_limit_bytes=LARGE_LIMIT),
+        compiler_params=pltpu.CompilerParams(vmem_limit_bytes=GROUP_LIMITS[group]),
         cost_estimate=pl.CostEstimate(
             flops=flops, bytes_accessed=8_000_000, transcendentals=rows * key_count
         ),
@@ -364,9 +367,10 @@
     entry_of = plan(block_lists, block_home, ctx_count, stored_blocks)
     held, query_rows, entry_of = lax.optimization_barrier((held, query_rows, entry_of))
 
-    outgoing = choose(
-        held.reshape(ctx_count * span, 640), width, ctx_count, groups, chosen, pair
-    )
+    held_rows = held.reshape(ctx_count * span, 640)
+    outgoing = [
+        choose(group, held_rows, width, ctx_count, chosen, pair) for group in range(groups)
+    ]
     keys0 = lax.all_to_all(outgoing[0], "ctx", split_axis=0, concat_axis=0, tiled=True)
     outgoing1, keys0 = lax.optimization_barrier((outgoing[1], keys0))
     keys1 = lax.all_to_all(outgoing1, "ctx", split_axis=0, concat_axis=0, tiled=True)

time: 164 us -> 162 us (0.988)
  blocking collectives: 23.9 us -> 0 us
  waiting for transfers between devices: 26.6 us -> 39.9 us
  starting transfers between devices: 56.1 us -> 63.2 us
  local copies, waits for them, and re-layouts: 12.9 us -> 14.6 us
    all_to_all x1 -> x0, blocking collectives: 23.9 us -> none  [local(): lax.all_to_all(outgoing[0], 'ctx', split_axis=0, concat_axis=0, tiled=True)]
    all_to_all x0 -> x1, waiting for transfers between devices: none -> 15.8 us  [local(): lax.all_to_all(outgoing[0], 'ctx', split_axis=0, concat_axis=0, tiled=True)]
    all_to_all x0 -> x1, starting transfers between devices: none -> 5.15 us  [local(): lax.all_to_all(outgoing[0], 'ctx', split_axis=0, concat_axis=0, tiled=True)]
    pallas_call x1 -> x2, Pallas kernels: 2.91 us -> 5.31 us  [choose(): pl.pallas_call(functools.partial(choose_kernel, group * chosen * pair //...]
    unnamed x50 -> x38, local copies, waits for them, and re-layouts: 9.39 us -> 9.35 us
  transfers between devices with their start and end apart: 24 -> 25, of which waited for: 12 -> 12; matrix products, arithmetic and copies ran while one was open for 9% -> 10% of each run, Pallas kernels for 18% -> 19%
where the time goes in v1:
time: 162 us; the launch traced here: 161 us
  starting transfers between devices  63.2 us (39%)
  waiting for transfers between devices  39.9 us (25%)
  Pallas kernels  38.2 us (24%)
  local copies, waits for them, and re-layouts  14.6 us (9%)
  other arithmetic  3.92 us (2%)
    ppermute x21, starting transfers between devices, shift(): lax.ppermute(x, 'head', [(i, (i + by) % count) for i in range(count)])  36.8 us
    pallas_call x2, Pallas kernels, group_grads(): pl.pallas_call(functools.partial(group_kernel, pieces), grid=(1,), in_spe...  25.4 us
    ppermute x21, waiting for transfers between devices, shift(): lax.ppermute(x, 'head', [(i, (i + by) % count) for i in range(count)])  15.8 us
    all_to_all x1, waiting for transfers between devices, local(): lax.all_to_all(outgoing[0], 'ctx', split_axis=0, concat_axis=0, tiled=True)  15.8 us
    unnamed x38, local copies, waits for them, and re-layouts  9.35 us
    all_to_all x1, starting transfers between devices, local(): lax.all_to_all(place(entry_of, by_group, share, pair), 'ctx', split_axis=...  7.91 us
    all_to_all x1, starting transfers between devices, local(): lax.all_to_all(spread_rows.reshape(ctx_count, span, 640), 'ctx', split_ax...  7.62 us
    all_to_all x1, waiting for transfers between devices, local(): lax.all_to_all(spread_rows.reshape(ctx_count, span, 640), 'ctx', split_ax...  6.86 us
  transfers between devices with their start and end apart: 25, of which 12 were waited for; matrix products, arithmetic and copies ran while one was open for 10% of the time, Pallas kernels for 19%

profile of v1, /device:TPU:2, one launch (start us, length us, event | category | flops | bytes accessed | tf_op | source)
XLA Modules:
  0.0 160.8 jit_solution(2155115728776290744)
XLA Ops:
  0.6 2.7 %spread.1 = bf16[512,640]{1,0:T(8,128)(2,1)} custom-call(s32[2,16]{1,0:T(2,128)} %lists_ref.3, s32[256]{0:T(256)} %home_ref.3, bf16[576,512]{1,0:T(8,128)(2,1)} %bitcast.89), custom_call_target="tpu_custom_call" | custom-call | tf_op jit(solution)/shard_map/spread/pallas_call | solution.py:89
  3.4 7.6 %all-to-all-start = ((bf16[32,16,640]{2,1,0:T(8,128)(2,1)}), bf16[32,16,640]{2,1,0:T(8,128)(2,1)S(1)}, u32[]{:S(2)}, u32[]{:S(2)}) async-start(bf16[32,16,640]{2,1,0:T(8,128)(2,1)} %bitcast.88), calls=%async_computation | async-start | bytes 1310720 | tf_op jit(solution)/shard_map/all_to_all | solution.py:362
  11.0 1.5 plan.1.index_ref
  12.5 3.5 %copy.10 = bf16[128,16,576]{2,1,0:T(8,128)(2,1)} copy(bf16[128,16,576]{0,2,1:T(8,128)(2,1)S(1)} %copy-done.3) | data formatting | bytes 4718592 | tf_op args[0]
  16.0 6.9 %all-to-all-done = bf16[32,16,640]{2,1,0:T(8,128)(2,1)S(1)} async-done(((bf16[32,16,640]{2,1,0:T(8,128)(2,1)}), bf16[32,16,640]{2,1,0:T(8,128)(2,1)S(1)}, u32[]{:S(2)}, u32[]{:S(2)}) %all-to-all-start) | async-done | bytes 655392 | tf_op jit(solution)/shard_map/all_to_all | solution.py:362
  22.9 2.1 %choose.3 = bf16[32,32,576]{2,1,0:T(8,128)(2,1)} custom-call(bf16[512,640]{1,0:T(8,128)(2,1)S(1)} %bitcast.80), custom_call_target="tpu_custom_call" | custom-call | flops 603979776 | bytes 2000000 | tf_op jit(solution)/shard_map/choose/pallas_call | solution.py:118
  25.0 5.2 %all-to-all-start.1 = ((bf16[32,32,576]{2,1,0:T(8,128)(2,1)}), bf16[32,32,576]{2,1,0:T(8,128)(2,1)S(1)}, u32[]{:S(2)}, u32[]{:S(2)}) async-start(bf16[32,32,576]{2,1,0:T(8,128)(2,1)} %choose.3), calls=%async_computation.1 | async-start | bytes 2621440 | tf_op jit(solution)/shard_map/all_to_all | solution.py:374
  30.2 3.2 %choose.2 = bf16[32,32,576]{2,1,0:T(8,128)(2,1)} custom-call(bf16[512,640]{1,0:T(8,128)(2,1)} %bitcast.81), custom_call_target="tpu_custom_call" | custom-call | flops 603979776 | bytes 2000000 | tf_op jit(solution)/shard_map/choose/pallas_call | solution.py:118
  33.4 15.8 %all-to-all-done.1.key_ref = bf16[32,32,576]{2,1,0:T(8,128)(2,1)S(1)} async-done(((bf16[32,32,576]{2,1,0:T(8,128)(2,1)}), bf16[32,32,576]{2,1,0:T(8,128)(2,1)S(1)}, u32[]{:S(2)}, u32[]{:S(2)}) %all-to-all-start.1) | async-done | bytes 1179680 | tf_op jit(solution)/shard_map/all_to_all | solution.py:374
  49.2 1.1 copy-done.4
  50.3 5.7 %all-to-all-start.2 = ((bf16[32,32,576]{2,1,0:T(8,128)(2,1)}), bf16[32,32,576]{2,1,0:T(8,128)(2,1)S(1)}, u32[]{:S(2)}, u32[]{:S(2)}) async-start(bf16[32,32,576]{2,1,0:T(8,128)(2,1)} %choose.2), calls=%async_computation.2 | async-start | bytes 2621440 | tf_op jit(solution)/shard_map/all_to_all | solution.py:376
  56.0 15.7 %group_grads.2 = (bf16[576,1024]{1,0:T(8,128)(2,1)}, f32[128,576]{1,0:T(8,128)}, bf16[128,576]{1,0:T(8,128)(2,1)}, bf16[128,576]{1,0:T(8,128)(2,1)}, bf16[128,57...) custom-call(s32[1]{0:T(128)} %bitcast.me_ref, ...), custom_call_target="tpu_custom_call" | custom-call | flops 5771362304 | bytes 8000000 | tf_op jit(solution)/shard_map/group_grads/pallas_call | solution.py:285
  71.7 1.9 %collective-permute-start = (bf16[128,576]{1,0:T(8,128)(2,1)}, bf16[128,576]{1,0:T(8,128)(2,1)S(1)}, u32[]{:S(2)}, u32[]{:S(2)}) collective-permute-start(bf16[128,576]{1,0:T(8,128)(2,1)} %get-tuple-element.40), channel_id=1, source_target_pairs={{0,1},{1,2},{2,3},{3,4},{4,5},{5,6},{6,7},{7,0},{8,9},{9,10},{10,1... | collective-permute-start | bytes 442376 | tf_op jit(solution)/shard_map/ppermute | solution.py:311
  73.7 4.2 %collective-permute-start.1 = (bf16[128,576]{1,0:T(8,128)(2,1)}, bf16[128,576]{1,0:T(8,128)(2,1)S(1)}, u32[]{:S(2)}, u32[]{:S(2)}) collective-permute-start(bf16[128,576]{1,0:T(8,128)(2,1)} %get-tuple-element.41), channel_id=1, source_target_pairs={{0,7},{1,0},{2,1},{3,2},{4,3},{5,4},{6,5},{7,6},{8,15},{9,8},{10,9... | collective-permute-start | bytes 442376 | tf_op jit(solution)/shard_map/ppermute | solution.py:311
  77.9 9.7 %group_grads.3 = (bf16[576,1024]{1,0:T(8,128)(2,1)S(1)}, f32[128,576]{1,0:T(8,128)S(1)}, bf16[128,576]{1,0:T(8,128)(2,1)S(1)}, bf16[128,576]{1,0:T(8,128)(2,1)S(...) custom-call(s32[1]{0:T(128)} %bitcast.me_ref, ...), custom_call_target="tpu_custom_call" | custom-call | flops 5771362304 | bytes 8000000 | tf_op jit(solution)/shard_map/group_grads/pallas_call | solution.py:285
  87.7 3.2 %collective-permute-start.10 = (bf16[128,576]{1,0:T(8,128)(2,1)S(1)}, bf16[128,576]{1,0:T(8,128)(2,1)S(1)}, u32[]{:S(2)}, u32[]{:S(2)}) collective-permute-start(bf16[128,576]{1,0:T(8,128)(2,1)S(1)} %get-tuple-element.53), channel_id=1, source_target_pairs={{0,7},{1,0},{2,1},{3,2},{4,3},{5,4},{6,5},{7,6},{8,15},{9,8},{10,9... | collective-permute-start | bytes 442376 | tf_op jit(solution)/shard_map/ppermute | solution.py:311
  90.9 1.9 %collective-permute-start.5 = (bf16[128,576]{1,0:T(8,128)(2,1)S(1)}, bf16[128,576]{1,0:T(8,128)(2,1)S(1)}, u32[]{:S(2)}, u32[]{:S(2)}) collective-permute-start(bf16[128,576]{1,0:T(8,128)(2,1)S(1)} %add_convert_fusion.6), channel_id=1, source_target_pairs={{0,7},{1,0},{2,1},{3,2},{4,3},{5,4},{6,5},{7,6},{8,15},{9,8},{10,9... | collective-permute-start | bytes 442376 | tf_op jit(solution)/shard_map/ppermute | solution.py:311
  92.9 0.3 collective-permute-start.2
  93.2 1.9 %collective-permute-done.7 = bf16[128,576]{1,0:T(8,128)(2,1)S(1)} collective-permute-done((bf16[128,576]{1,0:T(8,128)(2,1)S(1)}, bf16[128,576]{1,0:T(8,128)(2,1)S(1)}, u32[]{:S(2)}, u32[]{:S(2)}) %collective-permute-start.7) | collective-permute-done | bytes 147488 | tf_op jit(solution)/shard_map/ppermute | solution.py:311
  95.3 0.2 collective-permute-done.10
  95.5 3.8 %collective-permute-start.11 = (bf16[128,576]{1,0:T(8,128)(2,1)S(1)}, bf16[128,576]{1,0:T(8,128)(2,1)S(1)}, u32[]{:S(2)}, u32[]{:S(2)}) collective-permute-start(bf16[128,576]{1,0:T(8,128)(2,1)S(1)} %add_convert_fusion.2), channel_id=1, source_target_pairs={{0,7},{1,0},{2,1},{3,2},{4,3},{5,4},{6,5},{7,6},{8,15},{9,8},{10,9... | collective-permute-start | bytes 442376 | tf_op jit(solution)/shard_map/ppermute | solution.py:311
  99.3 2.6 %collective-permute-start.6 = (bf16[128,576]{1,0:T(8,128)(2,1)S(1)}, bf16[128,576]{1,0:T(8,128)(2,1)S(1)}, u32[]{:S(2)}, u32[]{:S(2)}) collective-permute-start(bf16[128,576]{1,0:T(8,128)(2,1)S(1)} %add_convert_fusion.5), channel_id=1, source_target_pairs={{0,7},{1,0},{2,1},{3,2},{4,3},{5,4},{6,5},{7,6},{8,15},{9,8},{10,9... | collective-permute-start | bytes 442376 | tf_op jit(solution)/shard_map/ppermute | solution.py:311
  102.0 0.3 collective-permute-start.3
  102.3 0.7 collective-permute-done.8
  103.2 0.1 collective-permute-done.11
  103.4 3.8 %collective-permute-start.12 = (bf16[128,576]{1,0:T(8,128)(2,1)S(1)}, bf16[128,576]{1,0:T(8,128)(2,1)S(1)}, u32[]{:S(2)}, u32[]{:S(2)}) collective-permute-start(bf16[128,576]{1,0:T(8,128)(2,1)S(1)} %add_convert_fusion.1), channel_id=1, source_target_pairs={{0,7},{1,0},{2,1},{3,2},{4,3},{5,4},{6,5},{7,6},{8,15},{9,8},{10,9... | collective-permute-start | bytes 442376 | tf_op jit(solution)/shard_map/ppermute | solution.py:311
  107.1 2.9 %collective-permute-done.3 = bf16[128,576]{1,0:T(8,128)(2,1)S(1)} collective-permute-done((bf16[128,576]{1,0:T(8,128)(2,1)S(1)}, bf16[128,576]{1,0:T(8,128)(2,1)S(1)}, u32[]{:S(2)}, u32[]{:S(2)}) %collective-permute-start.3) | collective-permute-done | bytes 147488 | tf_op jit(solution)/shard_map/ppermute | solution.py:311
  110.2 3.5 %collective-permute-start.13 = (bf16[128,576]{1,0:T(8,128)(2,1)S(1)}, bf16[128,576]{1,0:T(8,128)(2,1)S(1)}, u32[]{:S(2)}, u32[]{:S(2)}) collective-permute-start(bf16[128,576]{1,0:T(8,128)(2,1)S(1)} %add_convert_fusion), channel_id=1, source_target_pairs={{0,7},{1,0},{2,1},{3,2},{4,3},{5,4},{6,5},{7,6},{8,15},{9,8},{10,9... | collective-permute-start | bytes 442376 | tf_op jit(solution)/shard_map/ppermute | solution.py:311
  113.8 1.1 slice.3
  114.9 1.8 %collective-permute-done.4.refs_1_ = bf16[128,576]{1,0:T(8,128)(2,1)S(1)} collective-permute-done((bf16[128,576]{1,0:T(8,128)(2,1)S(1)}, bf16[128,576]{1,0:T(8,128)(2,1)S(1)}, u32[]{:S(2)}, u32[]{:S(2)}) %collective-permute-start.4) | collective-permute-done | bytes 147488 | tf_op jit(solution)/shard_map/ppermute | solution.py:311
  116.7 2.4 %place.1 = bf16[64,8,576]{2,1,0:T(8,128)(2,1)} custom-call(s32[64]{0:T(128)S(1)} %copy-done.2, f32[128,576]{1,0:T(8,128)S(1)} %copy-done.1, bf16[128,576]{1,0:T(8,128)(2,1)S(1)} %collective-permute-done.4.refs_1_, bf16[128,576]{1,0:T(8,128)(2,1)S(1)} %collective-permute-done.6.refs_2_, f32[128,576]{1,0:T(8,128)S(1)} %get-tuple-element.46.refs_3_, ...), custom_call_target="tpu_custom_call" | custom-call | tf_op jit(solution)/shard_map/place/pallas_call | solution.py:166
  119.1 7.9 %all-to-all-start.3 = ((bf16[64,8,576]{2,1,0:T(8,128)(2,1)}), bf16[64,8,576]{2,1,0:T(8,128)(2,1)S(1)}, u32[]{:S(2)}, u32[]{:S(2)}) async-start(bf16[64,8,576]{2,1,0:T(8,128)(2,1)} %place.1), calls=%async_computation.3 | async-start | bytes 1310720 | tf_op jit(solution)/shard_map/all_to_all | solution.py:393
  127.0 1.3 select_reduce_fusion.1
  128.5 2.4 %copy.11 = bf16[576,1024]{0,1:T(8,128)(2,1)} copy(bf16[576,1024]{1,0:T(8,128)(2,1)} %get-tuple-element.31) | data formatting | bytes 2359296 | tf_op jit(solution)/shard_map/group_grads/pallas_call | solution.py:285
  130.9 1.4 copy.12
  132.4 2.1 %pad_maximum_fusion = bf16[2,576,64,16]{1,3,2,0:T(8,128)(2,1)S(1)} fusion(bf16[1,576,64,16]{1,3,2,0:T(8,128)(2,1)} %bitcast.84, bf16[1,576,64,16]{1,3,2,0:T(8,128)(2,1)} %bitcast.83), kind=kLoop, calls=%fused_computation | loop fusion | flops 1179648 | bytes 4718592 | tf_op jit(solution)/shard_map/stack | solution.py:389
  134.5 3.1 %copy.15 = bf16[128,16,576]{0,2,1:T(8,128)(2,1)} copy(bf16[128,16,576]{2,1,0:T(8,128)(2,1)S(1)} %bitcast.82) | data formatting | bytes 4718592
  137.6 1.4 all-to-all-done.3.rows_ref
  138.9 0.9 gather_sum.1
  139.8 0.6 collective-permute-start.20
  140.4 4.8 %collective-permute-start.17 = (bf16[8,8,576]{2,1,0:T(8,128)(2,1)S(1)}, bf16[8,8,576]{2,1,0:T(8,128)(2,1)S(1)}, u32[]{:S(2)}, u32[]{:S(2)}) collective-permute-start(bf16[8,8,576]{2,1,0:T(8,128)(2,1)S(1)} %gather_sum.1), channel_id=1, source_target_pairs={{0,2},{1,3},{2,4},{3,5},{4,6},{5,7},{6,0},{7,1},{8,10},{9,11},{10,... | collective-permute-start | bytes 221192 | tf_op jit(solution)/shard_map/ppermute | solution.py:311
  145.2 1.4 collective-permute-start.14
  146.6 4.6 %collective-permute-done.17 = bf16[8,8,576]{2,1,0:T(8,128)(2,1)S(1)} collective-permute-done((bf16[8,8,576]{2,1,0:T(8,128)(2,1)S(1)}, bf16[8,8,576]{2,1,0:T(8,128)(2,1)S(1)}, u32[]{:S(2)}, u32[]{:S(2)}) %collective-permute-start.17) | collective-permute-done | bytes 73760 | tf_op jit(solution)/shard_map/ppermute | solution.py:311
  151.2 1.0 collective-permute-start.18
  152.2 3.2 %collective-permute-start.16 = (bf16[8,8,576]{2,1,0:T(8,128)(2,1)S(1)}, bf16[8,8,576]{2,1,0:T(8,128)(2,1)S(1)}, u32[]{:S(2)}, u32[]{:S(2)}) collective-permute-start(bf16[8,8,576]{2,1,0:T(8,128)(2,1)S(1)} %collective-permute-done.15), channel_id=1, source_target_pairs={{0,7},{1,0},{2,1},{3,2},{4,3},{5,4},{6,5},{7,6},{8,15},{9,8},{10,9... | collective-permute-start | bytes 221192 | tf_op jit(solution)/shard_map/ppermute | solution.py:311
  155.5 3.0 %collective-permute-done.16 = bf16[8,8,576]{2,1,0:T(8,128)(2,1)S(1)} collective-permute-done((bf16[8,8,576]{2,1,0:T(8,128)(2,1)S(1)}, bf16[8,8,576]{2,1,0:T(8,128)(2,1)S(1)}, u32[]{:S(2)}, u32[]{:S(2)}) %collective-permute-start.16) | collective-permute-done | bytes 73760 | tf_op jit(solution)/shard_map/ppermute | solution.py:311
  158.6 0.4 collective-permute-done.19
  159.4 1.4 copy.16
  (71 shorter events, 1.5 us)
Async XLA Ops:
  0.6 11.9 %copy-start.3 = (bf16[128,16,576]{0,2,1:T(8,128)(2,1)S(1)}, bf16[128,16,576]{0,2,1:T(8,128)(2,1)}, u32[]{:S(2)}) copy-start(bf16[128,16,576]{0,2,1:T(8,128)(2,1)} %param.5) | copy-start | bytes 7077892
  3.4 19.5 %all-to-all-start = ((bf16[32,16,640]{2,1,0:T(8,128)(2,1)}), bf16[32,16,640]{2,1,0:T(8,128)(2,1)S(1)}, u32[]{:S(2)}, u32[]{:S(2)}) async-start(bf16[32,16,640]{2,1,0:T(8,128)(2,1)} %bitcast.88), calls=%async_computation | async-start | bytes 1310720 | tf_op jit(solution)/shard_map/all_to_all | solution.py:362
  22.9 2.1 %copy-start = (bf16[32,16,640]{2,1,0:T(8,128)(2,1)}, bf16[32,16,640]{2,1,0:T(8,128)(2,1)S(1)}, u32[]{:S(2)}) copy-start(bf16[32,16,640]{2,1,0:T(8,128)(2,1)S(1)} %all-to-all-done) | copy-start | bytes 1966084
  25.0 24.2 %all-to-all-start.1 = ((bf16[32,32,576]{2,1,0:T(8,128)(2,1)}), bf16[32,32,576]{2,1,0:T(8,128)(2,1)S(1)}, u32[]{:S(2)}, u32[]{:S(2)}) async-start(bf16[32,32,576]{2,1,0:T(8,128)(2,1)} %choose.3), calls=%async_computation.1 | async-start | bytes 2621440 | tf_op jit(solution)/shard_map/all_to_all | solution.py:374
  49.2 1.1 copy-start.4
  50.3 27.6 %all-to-all-start.2 = ((bf16[32,32,576]{2,1,0:T(8,128)(2,1)}), bf16[32,32,576]{2,1,0:T(8,128)(2,1)S(1)}, u32[]{:S(2)}, u32[]{:S(2)}) async-start(bf16[32,32,576]{2,1,0:T(8,128)(2,1)} %choose.2), calls=%async_computation.2 | async-start | bytes 2621440 | tf_op jit(solution)/shard_map/all_to_all | solution.py:376
  71.7 19.1 %collective-permute-start = (bf16[128,576]{1,0:T(8,128)(2,1)}, bf16[128,576]{1,0:T(8,128)(2,1)S(1)}, u32[]{:S(2)}, u32[]{:S(2)}) collective-permute-start(bf16[128,576]{1,0:T(8,128)(2,1)} %get-tuple-element.40), channel_id=1, source_target_pairs={{0,1},{1,2},{2,3},{3,4},{4,5},{5,6},{6,7},{7,0},{8,9},{9,10},{10,1... | collective-permute-start | bytes 442376 | tf_op jit(solution)/shard_map/ppermute | solution.py:311
  73.7 17.2 %copy-start.9 = (bf16[128,576]{1,0:T(8,128)(2,1)S(1)}, bf16[128,576]{1,0:T(8,128)(2,1)}, u32[]{:S(2)}) copy-start(bf16[128,576]{1,0:T(8,128)(2,1)} %get-tuple-element.44) | copy-start | bytes 442372
  73.7 19.2 %copy-start.8 = (bf16[128,576]{1,0:T(8,128)(2,1)S(1)}, bf16[128,576]{1,0:T(8,128)(2,1)}, u32[]{:S(2)}) copy-start(bf16[128,576]{1,0:T(8,128)(2,1)} %get-tuple-element.38) | copy-start | bytes 442372
  73.7 17.2 %collective-permute-start.1 = (bf16[128,576]{1,0:T(8,128)(2,1)}, bf16[128,576]{1,0:T(8,128)(2,1)S(1)}, u32[]{:S(2)}, u32[]{:S(2)}) collective-permute-start(bf16[128,576]{1,0:T(8,128)(2,1)} %get-tuple-element.41), channel_id=1, source_target_pairs={{0,7},{1,0},{2,1},{3,2},{4,3},{5,4},{6,5},{7,6},{8,15},{9,8},{10,9... | collective-permute-start | bytes 442376 | tf_op jit(solution)/shard_map/ppermute | solution.py:311
  87.5 11.7 %copy-start.7 = (bf16[128,576]{1,0:T(8,128)(2,1)S(1)}, bf16[128,576]{1,0:T(8,128)(2,1)}, u32[]{:S(2)}) copy-start(bf16[128,576]{1,0:T(8,128)(2,1)} %get-tuple-element.43) | copy-start | bytes 442372
  87.6 14.4 %copy-start.6 = (bf16[128,576]{1,0:T(8,128)(2,1)S(1)}, bf16[128,576]{1,0:T(8,128)(2,1)}, u32[]{:S(2)}) copy-start(bf16[128,576]{1,0:T(8,128)(2,1)} %get-tuple-element.37) | copy-start | bytes 442372
  87.6 7.5 %collective-permute-start.7 = (bf16[128,576]{1,0:T(8,128)(2,1)S(1)}, bf16[128,576]{1,0:T(8,128)(2,1)S(1)}, u32[]{:S(2)}, u32[]{:S(2)}) collective-permute-start(bf16[128,576]{1,0:T(8,128)(2,1)S(1)} %get-tuple-element.49), channel_id=1, source_target_pairs={{0,1},{1,2},{2,3},{3,4},{4,5},{5,6},{6,7},{7,0},{8,9},{9,10},{10,1... | collective-permute-start | bytes 442376 | tf_op jit(solution)/shard_map/ppermute | solution.py:311
  87.7 7.8 %collective-permute-start.10 = (bf16[128,576]{1,0:T(8,128)(2,1)S(1)}, bf16[128,576]{1,0:T(8,128)(2,1)S(1)}, u32[]{:S(2)}, u32[]{:S(2)}) collective-permute-start(bf16[128,576]{1,0:T(8,128)(2,1)S(1)} %get-tuple-element.53), channel_id=1, source_target_pairs={{0,7},{1,0},{2,1},{3,2},{4,3},{5,4},{6,5},{7,6},{8,15},{9,8},{10,9... | collective-permute-start | bytes 442376 | tf_op jit(solution)/shard_map/ppermute | solution.py:311
  90.9 8.3 %collective-permute-start.5 = (bf16[128,576]{1,0:T(8,128)(2,1)S(1)}, bf16[128,576]{1,0:T(8,128)(2,1)S(1)}, u32[]{:S(2)}, u32[]{:S(2)}) collective-permute-start(bf16[128,576]{1,0:T(8,128)(2,1)S(1)} %add_convert_fusion.6), channel_id=1, source_target_pairs={{0,7},{1,0},{2,1},{3,2},{4,3},{5,4},{6,5},{7,6},{8,15},{9,8},{10,9... | collective-permute-start | bytes 442376 | tf_op jit(solution)/shard_map/ppermute | solution.py:311
  92.9 9.1 %collective-permute-start.2 = (bf16[128,576]{1,0:T(8,128)(2,1)S(1)}, bf16[128,576]{1,0:T(8,128)(2,1)S(1)}, u32[]{:S(2)}, u32[]{:S(2)}) collective-permute-start(bf16[128,576]{1,0:T(8,128)(2,1)S(1)} %add_convert_fusion.9), channel_id=1, source_target_pairs={{0,1},{1,2},{2,3},{3,4},{4,5},{5,6},{6,7},{7,0},{8,9},{9,10},{10,1... | collective-permute-start | bytes 442376 | tf_op jit(solution)/shard_map/ppermute | solution.py:311
  95.2 14.9 %copy-start.5 = (bf16[128,576]{1,0:T(8,128)(2,1)S(1)}, bf16[128,576]{1,0:T(8,128)(2,1)}, u32[]{:S(2)}) copy-start(bf16[128,576]{1,0:T(8,128)(2,1)} %get-tuple-element.36) | copy-start | bytes 442372
  95.2 7.9 %collective-permute-start.8 = (bf16[128,576]{1,0:T(8,128)(2,1)S(1)}, bf16[128,576]{1,0:T(8,128)(2,1)S(1)}, u32[]{:S(2)}, u32[]{:S(2)}) collective-permute-start(bf16[128,576]{1,0:T(8,128)(2,1)S(1)} %add_convert_fusion.4), channel_id=1, source_target_pairs={{0,1},{1,2},{2,3},{3,4},{4,5},{5,6},{6,7},{7,0},{8,9},{9,10},{10,1... | collective-permute-start | bytes 442376 | tf_op jit(solution)/shard_map/ppermute | solution.py:311
  95.5 7.8 %collective-permute-start.11 = (bf16[128,576]{1,0:T(8,128)(2,1)S(1)}, bf16[128,576]{1,0:T(8,128)(2,1)S(1)}, u32[]{:S(2)}, u32[]{:S(2)}) collective-permute-start(bf16[128,576]{1,0:T(8,128)(2,1)S(1)} %add_convert_fusion.2), channel_id=1, source_target_pairs={{0,7},{1,0},{2,1},{3,2},{4,3},{5,4},{6,5},{7,6},{8,15},{9,8},{10,9... | collective-permute-start | bytes 442376 | tf_op jit(solution)/shard_map/ppermute | solution.py:311
  99.3 15.5 %collective-permute-start.6 = (bf16[128,576]{1,0:T(8,128)(2,1)S(1)}, bf16[128,576]{1,0:T(8,128)(2,1)S(1)}, u32[]{:S(2)}, u32[]{:S(2)}) collective-permute-start(bf16[128,576]{1,0:T(8,128)(2,1)S(1)} %add_convert_fusion.5), channel_id=1, source_target_pairs={{0,7},{1,0},{2,1},{3,2},{4,3},{5,4},{6,5},{7,6},{8,15},{9,8},{10,9... | collective-permute-start | bytes 442376 | tf_op jit(solution)/shard_map/ppermute | solution.py:311
  101.9 14.8 %copy-start.1 = (f32[128,576]{1,0:T(8,128)S(1)}, f32[128,576]{1,0:T(8,128)}, u32[]{:S(2)}) copy-start(f32[128,576]{1,0:T(8,128)} %get-tuple-element.35.refs_0_) | copy-start | bytes 884740
  101.9 14.8 %copy-start.2 = (s32[64]{0:T(128)S(1)}, s32[64]{0:T(128)}, u32[]{:S(2)}) copy-start(s32[64]{0:T(128)} %plan.1.index_ref) | copy-start | bytes 772
  102.0 8.1 %collective-permute-start.3 = (bf16[128,576]{1,0:T(8,128)(2,1)S(1)}, bf16[128,576]{1,0:T(8,128)(2,1)S(1)}, u32[]{:S(2)}, u32[]{:S(2)}) collective-permute-start(bf16[128,576]{1,0:T(8,128)(2,1)S(1)} %add_convert_fusion.8), channel_id=1, source_target_pairs={{0,1},{1,2},{2,3},{3,4},{4,5},{5,6},{6,7},{7,0},{8,9},{9,10},{10,1... | collective-permute-start | bytes 442376 | tf_op jit(solution)/shard_map/ppermute | solution.py:311
  103.1 11.8 %collective-permute-start.9 = (bf16[128,576]{1,0:T(8,128)(2,1)S(1)}, bf16[128,576]{1,0:T(8,128)(2,1)S(1)}, u32[]{:S(2)}, u32[]{:S(2)}) collective-permute-start(bf16[128,576]{1,0:T(8,128)(2,1)S(1)} %add_convert_fusion.3), channel_id=1, source_target_pairs={{0,1},{1,2},{2,3},{3,4},{4,5},{5,6},{6,7},{7,0},{8,9},{9,10},{10,1... | collective-permute-start | bytes 442376 | tf_op jit(solution)/shard_map/ppermute | solution.py:311
  103.4 6.8 %collective-permute-start.12 = (bf16[128,576]{1,0:T(8,128)(2,1)S(1)}, bf16[128,576]{1,0:T(8,128)(2,1)S(1)}, u32[]{:S(2)}, u32[]{:S(2)}) collective-permute-start(bf16[128,576]{1,0:T(8,128)(2,1)S(1)} %add_convert_fusion.1), channel_id=1, source_target_pairs={{0,7},{1,0},{2,1},{3,2},{4,3},{5,4},{6,5},{7,6},{8,15},{9,8},{10,9... | collective-permute-start | bytes 442376 | tf_op jit(solution)/shard_map/ppermute | solution.py:311
  110.1 6.6 %collective-permute-start.4 = (bf16[128,576]{1,0:T(8,128)(2,1)S(1)}, bf16[128,576]{1,0:T(8,128)(2,1)S(1)}, u32[]{:S(2)}, u32[]{:S(2)}) collective-permute-start(bf16[128,576]{1,0:T(8,128)(2,1)S(1)} %add_convert_fusion.7), channel_id=1, source_target_pairs={{0,1},{1,2},{2,3},{3,4},{4,5},{5,6},{6,7},{7,0},{8,9},{9,10},{10,1... | collective-permute-start | bytes 442376 | tf_op jit(solution)/shard_map/ppermute | solution.py:311
  110.2 6.5 %collective-permute-start.13 = (bf16[128,576]{1,0:T(8,128)(2,1)S(1)}, bf16[128,576]{1,0:T(8,128)(2,1)S(1)}, u32[]{:S(2)}, u32[]{:S(2)}) collective-permute-start(bf16[128,576]{1,0:T(8,128)(2,1)S(1)} %add_convert_fusion), channel_id=1, source_target_pairs={{0,7},{1,0},{2,1},{3,2},{4,3},{5,4},{6,5},{7,6},{8,15},{9,8},{10,9... | collective-permute-start | bytes 442376 | tf_op jit(solution)/shard_map/ppermute | solution.py:311
  119.1 19.8 %all-to-all-start.3 = ((bf16[64,8,576]{2,1,0:T(8,128)(2,1)}), bf16[64,8,576]{2,1,0:T(8,128)(2,1)S(1)}, u32[]{:S(2)}, u32[]{:S(2)}) async-start(bf16[64,8,576]{2,1,0:T(8,128)(2,1)} %place.1), calls=%async_computation.3 | async-start | bytes 1310720 | tf_op jit(solution)/shard_map/all_to_all | solution.py:393
  139.8 19.2 %collective-permute-start.20 = (bf16[8,8,576]{2,1,0:T(8,128)(2,1)S(1)}, bf16[8,8,576]{2,1,0:T(8,128)(2,1)S(1)}, u32[]{:S(2)}, u32[]{:S(2)}) collective-permute-start(bf16[8,8,576]{2,1,0:T(8,128)(2,1)S(1)} %gather_sum.1), channel_id=1, source_target_pairs={{0,1},{1,2},{2,3},{3,4},{4,5},{5,6},{6,7},{7,0},{8,9},{9,10},{10,1... | collective-permute-start | bytes 221192 | tf_op jit(solution)/shard_map/ppermute | solution.py:311
  140.4 10.8 %collective-permute-start.17 = (bf16[8,8,576]{2,1,0:T(8,128)(2,1)S(1)}, bf16[8,8,576]{2,1,0:T(8,128)(2,1)S(1)}, u32[]{:S(2)}, u32[]{:S(2)}) collective-permute-start(bf16[8,8,576]{2,1,0:T(8,128)(2,1)S(1)} %gather_sum.1), channel_id=1, source_target_pairs={{0,2},{1,3},{2,4},{3,5},{4,6},{5,7},{6,0},{7,1},{8,10},{9,11},{10,... | collective-permute-start | bytes 221192 | tf_op jit(solution)/shard_map/ppermute | solution.py:311
  145.2 7.0 %collective-permute-start.15 = (bf16[8,8,576]{2,1,0:T(8,128)(2,1)S(1)}, bf16[8,8,576]{2,1,0:T(8,128)(2,1)S(1)}, u32[]{:S(2)}, u32[]{:S(2)}) collective-permute-start(bf16[8,8,576]{2,1,0:T(8,128)(2,1)S(1)} %gather_sum.1), channel_id=1, source_target_pairs={{0,6},{1,7},{2,0},{3,1},{4,2},{5,3},{6,4},{7,5},{8,14},{9,15},{10,... | collective-permute-start | bytes 221192 | tf_op jit(solution)/shard_map/ppermute | solution.py:311
  145.2 10.2 %collective-permute-start.14 = (bf16[8,8,576]{2,1,0:T(8,128)(2,1)S(1)}, bf16[8,8,576]{2,1,0:T(8,128)(2,1)S(1)}, u32[]{:S(2)}, u32[]{:S(2)}) collective-permute-start(bf16[8,8,576]{2,1,0:T(8,128)(2,1)S(1)} %gather_sum.1), channel_id=1, source_target_pairs={{0,7},{1,0},{2,1},{3,2},{4,3},{5,4},{6,5},{7,6},{8,15},{9,8},{10,9... | collective-permute-start | bytes 221192 | tf_op jit(solution)/shard_map/ppermute | solution.py:311
  151.2 7.8 %collective-permute-start.19 = (bf16[8,8,576]{2,1,0:T(8,128)(2,1)S(1)}, bf16[8,8,576]{2,1,0:T(8,128)(2,1)S(1)}, u32[]{:S(2)}, u32[]{:S(2)}) collective-permute-start(bf16[8,8,576]{2,1,0:T(8,128)(2,1)S(1)} %collective-permute-done.17), channel_id=1, source_target_pairs={{0,1},{1,2},{2,3},{3,4},{4,5},{5,6},{6,7},{7,0},{8,9},{9,10},{10,1... | collective-permute-start | bytes 221192 | tf_op jit(solution)/shard_map/ppermute | solution.py:311
  151.2 7.3 %collective-permute-start.18 = (bf16[8,8,576]{2,1,0:T(8,128)(2,1)S(1)}, bf16[8,8,576]{2,1,0:T(8,128)(2,1)S(1)}, u32[]{:S(2)}, u32[]{:S(2)}) collective-permute-start(bf16[8,8,576]{2,1,0:T(8,128)(2,1)S(1)} %collective-permute-done.17), channel_id=1, source_target_pairs={{0,2},{1,3},{2,4},{3,5},{4,6},{5,7},{6,0},{7,1},{8,10},{9,11},{10,... | collective-permute-start | bytes 221192 | tf_op jit(solution)/shard_map/ppermute | solution.py:311
  152.2 6.3 %collective-permute-start.16 = (bf16[8,8,576]{2,1,0:T(8,128)(2,1)S(1)}, bf16[8,8,576]{2,1,0:T(8,128)(2,1)S(1)}, u32[]{:S(2)}, u32[]{:S(2)}) collective-permute-start(bf16[8,8,576]{2,1,0:T(8,128)(2,1)S(1)} %collective-permute-done.15), channel_id=1, source_target_pairs={{0,7},{1,0},{2,1},{3,2},{4,3},{5,4},{6,5},{7,6},{8,15},{9,8},{10,9... | collective-permute-start | bytes 221192 | tf_op jit(solution)/shard_map/ppermute | solution.py:311
